TPU v7x, 32 devices: a whole 2x2x4 slice. The times are simulated.
32 devices in a mesh: ctx: 4 (over z), head: 2 (over x), rep: 4 (over y, core).
Axes of the slice: x: 2, y: 2, z: 4, core: 2. Of those that a mesh axis runs over, the one named last changes fastest.
Arguments:
- trunk_query_array: bfloat16 [2048, 8192], P(('rep', 'ctx'), 'head'), parts along dimension 0, may hold values from -200 to 200
- trunk_key_array: bfloat16 [2048, 1024], P(('rep', 'ctx'), 'head'), parts along dimension 0, may hold values from -6 to 6
- trunk_value_array: bfloat16 [2048, 1024], P(('rep', 'ctx'), 'head'), parts along dimension 0, may hold values from -15 to 15
- tree_query_array: bfloat16 [40960, 8192], P(('rep', 'ctx'), 'head'), parts along dimension 0, may hold values from -200 to 200
- tree_key_array: bfloat16 [40960, 1024], P(('rep', 'ctx'), 'head'), parts along dimension 0, may hold values from -6 to 6
- tree_value_array: bfloat16 [40960, 1024], P(('rep', 'ctx'), 'head'), parts along dimension 0, may hold values from -15 to 15
- ancestors: int32 [320, 2], P('rep'), parts along dimension 0, may hold values from -1 to 79, as said below
Outputs:
- trunk_out: bfloat16 [2048, 8192], P(('rep', 'ctx'), 'head'), parts along dimension 0
- tree_out: bfloat16 [40960, 8192], P(('rep', 'ctx'), 'head'), parts along dimension 0
There are 4 independent parts, one for each index of `rep`. A program takes and returns all parts, laid end to end along the dimension named above; each array names one. Nothing has to cross between parts.
Inputs may be any that keep to these rules, and one draw needn't show every extreme that they name: `ancestors`: row s holds the slot of the grandparent and of the parent of the segment in slot s, -1 where there is none. The segments form a tree: 16 segments below the trunk, 2 children under each, 1 leaf child under each of those; slots 20 * c to 20 * c + 19 lie on index c of ctx, and the segments are placed on slots in any order, except that slot 79 always holds a segment that has children. No index of ctx holds more than 16 segments that have children, and some index holds exactly 16.
All inputs are finite; a program needn't handle non-finite values.
Results may differ from a plain program's by a relative error of at most 0.0045.
Values may be sent and summed in bfloat16 or wider, within the bound.
A program may use at most 320 MiB of HBM per device.

v0:
```python
import math

import jax
import jax.numpy as jnp
from jax import lax
from jax.sharding import PartitionSpec as P

HEAD_SIZE = 128
SEGMENT_TOKENS = 128


masked_score = -1e30


def absorb(running, scores, allowed, value_rows):
    peak, totals, weighted = running
    if allowed is not None:
        scores = jnp.where(allowed, scores, masked_score)
    new_peak = jnp.maximum(peak, jnp.max(scores, axis=-1))
    factor = jnp.exp(peak - new_peak)
    weights = jnp.exp(scores - new_peak[..., None])
    if allowed is not None:
        weights = jnp.where(allowed, weights, 0.0)
    totals = totals * factor + jnp.sum(weights, axis=-1)
    update = jnp.einsum(
        "rhgk,khd->rhgd",
        weights.astype(jnp.bfloat16),
        value_rows,
        preferred_element_type=jnp.float32,
    )
    weighted = weighted * factor[..., None] + update
    return (new_peak, totals, weighted)


def local_part(inputs):
    queries, key_rows, value_rows, allowed = inputs
    inverse_root = 1.0 / math.sqrt(HEAD_SIZE)
    scores = (
        jnp.einsum("rhgd,khd->rhgk", queries, key_rows, preferred_element_type=jnp.float32)
        * inverse_root
    )
    allowed_full = allowed[:, None, None, :]
    scores = jnp.where(allowed_full, scores, masked_score)
    peak = jnp.max(scores, axis=-1)
    weights = jnp.where(allowed_full, jnp.exp(scores - peak[..., None]), 0.0)
    totals = jnp.sum(weights, axis=-1)
    weighted = jnp.einsum(
        "rhgk,khd->rhgd",
        weights.astype(jnp.bfloat16),
        value_rows,
        preferred_element_type=jnp.float32,
    )
    return (peak, totals, weighted)


def finish(running, row_total, block_width):
    peak, totals, weighted = running
    return (weighted / totals[..., None]).astype(jnp.bfloat16).reshape(row_total, block_width)


def local(
    trunk_query_array,
    trunk_key_array,
    trunk_value_array,
    tree_query_array,
    tree_key_array,
    tree_value_array,
    ancestors,
):
    own_index = lax.axis_index("ctx")
    inverse_root = 1.0 / math.sqrt(HEAD_SIZE)
    trunk_rows = trunk_query_array.shape[0]
    query_heads = trunk_query_array.shape[1] // HEAD_SIZE
    key_heads = trunk_key_array.shape[1] // HEAD_SIZE
    query_group_size = query_heads // key_heads
    slot_count = tree_query_array.shape[0] // SEGMENT_TOKENS
    tree_rows = slot_count * SEGMENT_TOKENS
    tree_queries = tree_query_array.reshape(
        slot_count, SEGMENT_TOKENS, key_heads, query_group_size, HEAD_SIZE
    )
    tree_key_rows = tree_key_array.reshape(slot_count, SEGMENT_TOKENS, key_heads, HEAD_SIZE)
    tree_value_rows = tree_value_array.reshape(slot_count, SEGMENT_TOKENS, key_heads, HEAD_SIZE)
    own_lists = lax.dynamic_slice_in_dim(ancestors, own_index * slot_count, slot_count, 0)
    present = own_lists >= 0
    picked_rows = jnp.maximum(own_lists, 0)
    every_key, every_value = (
        lax.all_gather(tree_key_array, "ctx", axis=0, tiled=True),
        lax.all_gather(tree_value_array, "ctx", axis=0, tiled=True),
    )
    every_key = every_key.reshape(-1, SEGMENT_TOKENS, key_heads, HEAD_SIZE)
    every_value = every_value.reshape(-1, SEGMENT_TOKENS, key_heads, HEAD_SIZE)
    fetched_keys = every_key[picked_rows].reshape(
        slot_count, 2 * SEGMENT_TOKENS, key_heads, HEAD_SIZE
    )
    fetched_values = every_value[picked_rows].reshape(
        slot_count, 2 * SEGMENT_TOKENS, key_heads, HEAD_SIZE
    )
    all_keys = jnp.concatenate([fetched_keys, tree_key_rows], axis=1)
    all_values = jnp.concatenate([fetched_values, tree_value_rows], axis=1)
    offsets = jnp.arange(SEGMENT_TOKENS, dtype=jnp.int32)
    self_allowed = jnp.broadcast_to(
        offsets[:, None] >= offsets[None, :], (slot_count, SEGMENT_TOKENS, SEGMENT_TOKENS)
    )
    first_seen = jnp.broadcast_to(
        present[:, 0][:, None, None], (slot_count, SEGMENT_TOKENS, SEGMENT_TOKENS)
    )
    second_seen = jnp.broadcast_to(
        present[:, 1][:, None, None], (slot_count, SEGMENT_TOKENS, SEGMENT_TOKENS)
    )
    allowed = jnp.concatenate([first_seen, second_seen, self_allowed], axis=2)
    tree_peak, tree_totals, tree_weighted = lax.map(
        local_part, (tree_queries, all_keys, all_values, allowed)
    )
    tree_state = (
        tree_peak.reshape(tree_rows, key_heads, query_group_size),
        tree_totals.reshape(tree_rows, key_heads, query_group_size),
        tree_weighted.reshape(tree_rows, key_heads, query_group_size, HEAD_SIZE),
    )
    trunk_state = (
        jnp.full((trunk_rows, key_heads, query_group_size), masked_score, jnp.float32),
        jnp.zeros((trunk_rows, key_heads, query_group_size), jnp.float32),
        jnp.zeros((trunk_rows, key_heads, query_group_size, HEAD_SIZE), jnp.float32),
    )
    trunk_queries = trunk_query_array.reshape(trunk_rows, key_heads, query_group_size, HEAD_SIZE)
    flat_queries = tree_query_array.reshape(tree_rows, key_heads, query_group_size, HEAD_SIZE)
    query_positions = own_index * trunk_rows + jnp.arange(trunk_rows, dtype=jnp.int32)
    key_piece = lax.all_gather(trunk_key_array, "ctx", axis=0, tiled=True)
    value_piece = lax.all_gather(trunk_value_array, "ctx", axis=0, tiled=True)
    key_count = key_piece.shape[0]
    block_size = math.gcd(key_count, 128)
    block_total = key_count // block_size
    key_blocks = key_piece.reshape(block_total, block_size, key_heads, HEAD_SIZE)
    value_blocks = value_piece.reshape(block_total, block_size, key_heads, HEAD_SIZE)
    key_positions = jnp.arange(key_count, dtype=jnp.int32).reshape(block_total, block_size)

    def scan_step(states, inputs):
        block_keys, block_values, block_positions = inputs
        trunk_running, tree_running = states
        trunk_scores = (
            jnp.einsum(
                "rhgd,khd->rhgk", trunk_queries, block_keys, preferred_element_type=jnp.float32
            )
            * inverse_root
        )
        trunk_allowed = (query_positions[:, None] >= block_positions[None, :])[:, None, None, :]
        trunk_running = absorb(trunk_running, trunk_scores, trunk_allowed, block_values)
        tree_scores = (
            jnp.einsum(
                "rhgd,khd->rhgk", flat_queries, block_keys, preferred_element_type=jnp.float32
            )
            * inverse_root
        )
        tree_running = absorb(tree_running, tree_scores, None, block_values)
        return ((trunk_running, tree_running), None)

    result, unused = lax.scan(
        scan_step, (trunk_state, tree_state), (key_blocks, value_blocks, key_positions)
    )
    trunk_final, tree_final = result
    trunk_out = finish(trunk_final, trunk_rows, query_heads * HEAD_SIZE)
    tree_out = finish(tree_final, tree_rows, query_heads * HEAD_SIZE)
    return (trunk_out, tree_out)


def solution(mesh):
    placed = (
        P(("rep", "ctx"), "head"),
        P(("rep", "ctx"), "head"),
        P(("rep", "ctx"), "head"),
        P(("rep", "ctx"), "head"),
        P(("rep", "ctx"), "head"),
        P(("rep", "ctx"), "head"),
        P("rep", None),
    )
    return jax.shard_map(
        local,
        mesh=mesh,
        in_specs=placed,
        out_specs=(P(("rep", "ctx"), "head"), P(("rep", "ctx"), "head")),
        check_vma=False,
    )
```

profile of v0, /device:TPU:0, one launch (start us, length us, event | category | flops | bytes accessed | tf_op | source)
XLA Modules:
  0.0 1186.0 jit_solution(11006980838773064412)
XLA Ops:
  8.7 5.0 reshape.96
  13.7 4.9 reshape.100
  18.9 30.9 %all_gather.14 = bf16[512,512]{1,0:T(8,128)(2,1)S(1)} all-gather(bf16[128,512]{1,0:T(8,128)(2,1)S(1)} %copy-done.13), channel_id=1, replica_groups=mesh['ctx'=4,'head'=2,'rep'=4] {'ctx'}, dimensions={0}, use_global_device_ids=true | all-gather | bytes 655360 | tf_op jit(solution)/shard_map/all_gather | solution.py:127
  50.8 23.2 %all_gather.15 = bf16[512,512]{1,0:T(8,128)(2,1)S(1)} all-gather(bf16[128,512]{1,0:T(8,128)(2,1)S(1)} %copy-done.14), channel_id=1, replica_groups=mesh['ctx'=4,'head'=2,'rep'=4] {'ctx'}, dimensions={0}, use_global_device_ids=true | all-gather | bytes 655360 | tf_op jit(solution)/shard_map/all_gather | solution.py:128
  76.8 4.0 copy.69
  80.8 3.9 copy.73
  84.7 26.2 %copy.81 = bf16[2560,4096]{0,1:T(8,128)(2,1)} copy(bf16[2560,4096]{1,0:T(8,128)(2,1)} %param.14) | data formatting | bytes 41943040 | tf_op args[3]
  110.9 18.8 %copy.113 = bf16[320,8,32,128]{3,2,1,0:T(8,128)(2,1)} copy(bf16[320,8,32,128]{3,1,2,0:T(8,128)(2,1)} %bitcast.161) | data formatting | bytes 41943040
  129.8 26.0 %copy.86 = bf16[2560,4,8,128]{3,0,2,1:T(8,128)(2,1)} copy(bf16[2560,4,8,128]{0,3,2,1:T(8,128)(2,1)} %bitcast.163) | data formatting | bytes 41943040
  156.4 55.1 %all-gather.3.cloned.1.call-done = bf16[10240,512]{1,0:T(8,128)(2,1)} async-done(((bf16[2560,512]{1,0:T(8,128)(2,1)}), bf16[10240,512]{1,0:T(8,128)(2,1)}) %all-gather.3.cloned.1.call-update) | async-done | bytes 10485776 | tf_op jit(solution)/shard_map/all_gather | solution.py:87
  211.6 15.8 %reshape.139 = bf16[80,128,4,128]{3,2,1,0:T(4,128)(2,1)} reshape(bf16[10240,512]{1,0:T(8,128)(2,1)} %all-gather.3.cloned.1.call-done) | data formatting | bytes 20971520 | tf_op jit(solution)/shard_map/reshape | solution.py:90
  227.4 11.1 copy.67
  238.4 157.8 %all-gather.5.cloned.1.call-done = bf16[10240,512]{1,0:T(8,128)(2,1)} async-done(((bf16[2560,512]{1,0:T(8,128)(2,1)}), bf16[10240,512]{1,0:T(8,128)(2,1)}) %all-gather.5.cloned.1.call-update) | async-done | bytes 10485776 | tf_op jit(solution)/shard_map/all_gather | solution.py:88
  396.2 15.3 %reshape.140 = bf16[80,128,4,128]{3,2,1,0:T(4,128)(2,1)} reshape(bf16[10240,512]{1,0:T(8,128)(2,1)} %all-gather.5.cloned.1.call-done) | data formatting | bytes 20971520 | tf_op jit(solution)/shard_map/reshape | solution.py:91
  411.6 11.0 copy.71
  422.6 8.7 gather_fusion.1
  431.2 8.5 gather_fusion
  439.7 3.8 copy.68
  446.3 5.7 pad_maximum_fusion
  452.0 275.2 %while.35 = (s32[]{:T(128)}, f32[20,128,4,8]{1,3,0,2:T(8,128)S(1)}, f32[20,128,4,8]{1,3,0,2:T(8,128)}, f32[20,128,4,8,128]{4,3,2,1,0:T(8,128)}, pred[20,128,384]...) while((s32[]{:T(128)}, f32[20,128,4,8]{1,3,0,2:T(8,128)S(1)}, ...), condition=%wide.region_3.4_spmd, body=%wide.region_0.3_spmd.sunk | while | flops 825745408 | bytes 33669244 | solution.py:111
  457.3 4.0 fusion.68
  471.0 4.0 fusion.68
  480.8 2.4 fusion.66
  484.8 4.0 fusion.68
  498.5 4.0 fusion.68
  512.3 4.0 fusion.68
  526.1 4.0 fusion.68
  539.9 4.0 fusion.68
  549.7 2.4 fusion.66
  553.7 4.0 fusion.68
  563.4 2.4 fusion.66
  567.4 4.0 fusion.68
  581.2 4.0 fusion.68
  590.9 2.4 fusion.66
  594.9 4.0 fusion.68
  604.7 2.4 fusion.66
  608.7 4.0 fusion.68
  622.4 4.0 fusion.68
  636.2 4.0 fusion.68
  650.0 4.0 fusion.68
  663.8 4.0 fusion.68
  673.5 2.4 fusion.66
  677.5 4.0 fusion.68
  687.2 2.4 fusion.66
  691.2 4.0 fusion.68
  705.0 4.0 fusion.68
  714.8 2.4 fusion.66
  718.7 4.0 fusion.68
  728.0 39.2 %copy.82 = f32[2560,4,8,128]{0,3,2,1:T(8,128)} copy(f32[2560,4,8,128]{3,2,1,0:T(8,128)} %bitcast.164) | data formatting | bytes 83886080
  767.2 359.2 %while.36 = (s32[]{:T(128)}, f32[128,4,8]{0,2,1:T(8,128)S(1)}, f32[128,4,8]{0,2,1:T(8,128)S(1)}, f32[128,4,8,128]{0,3,2,1:T(8,128)S(1)}, f32[2560,4,8]{0,2,1:T(8...) while((s32[]{:T(128)}, f32[128,4,8]{0,2,1:T(8,128)S(1)}, ...), condition=%wide.region_9.10_spmd.clone, body=%wide.region_4.9_spmd.clone.sunk | while | flops 5750591488 | bytes 253561648 | solution.py:156
  772.3 21.2 %bitcast_reduce_fusion.2 = (f32[2560,4,8]{0,2,1:T(8,128)}, f32[4,128,2560,8]{2,1,3,0:T(8,128)}) fusion(bf16[2560,4,8,128]{3,0,2,1:T(8,128)(2,1)} %get-tuple-element.515, bf16[1,128,4,128]{3,2,1,0:T(4,128)(2,1)S(1)} %get-tuple-element.437), kind=kOutput, calls=%fused_computation.29.clone.1 | convolution fusion | flops 2705244160 | bytes 63373312 | tf_op jit(solution)/shard_map/while/body/eval_jaxpr/rhgd,khd->rhgk/dot_general | solution.py:148
  794.6 17.1 %fusion.79 = f32[2560,4,8]{0,2,1:T(8,128)S(1)} fusion(f32[4,128,2560,8]{2,1,3,0:T(8,128)} %get-tuple-element.444, f32[2560,4,8]{0,2,1:T(8,128)S(1)} %max.17), kind=kLoop, calls=%fused_computation.32.clone.1 | loop fusion | flops 31375360 | bytes 42598400 | tf_op jit(solution)/shard_map/while/body/eval_jaxpr/reduce_sum | solution.py:24
  813.4 42.8 %bitcast_add_fusion.5 = f32[2560,4,8,128]{0,3,2,1:T(8,128)} fusion(f32[2560,4,8,128]{0,3,2,1:T(8,128)} %get-tuple-element.495, f32[4,128,2560,8]{2,1,3,0:T(8,128)} %get-tuple-element.444, f32[2560,4,8]{0,2,1:T(8,128)} %get-tuple-element.446, f32[2560,4,8]{0,2,1:T(8,128)S(1)} %max.17, bf16[1,128,4,128]{1,3,2,0:T(8,128)(2,1)} %copy-done.4), kind=kOutput, calls=%fused_computation.27.clone.1 | convolution fusion | flops 2736783360 | bytes 126615552 | tf_op jit(solution)/shard_map/while/body/eval_jaxpr/rhgk,khd->rhgd/dot_general | solution.py:25
  862.0 21.2 %bitcast_reduce_fusion.2 = (f32[2560,4,8]{0,2,1:T(8,128)}, f32[4,128,2560,8]{2,1,3,0:T(8,128)}) fusion(bf16[2560,4,8,128]{3,0,2,1:T(8,128)(2,1)} %get-tuple-element.515, bf16[1,128,4,128]{3,2,1,0:T(4,128)(2,1)S(1)} %get-tuple-element.437), kind=kOutput, calls=%fused_computation.29.clone.1 | convolution fusion | flops 2705244160 | bytes 63373312 | tf_op jit(solution)/shard_map/while/body/eval_jaxpr/rhgd,khd->rhgk/dot_general | solution.py:148
  884.4 17.1 %fusion.79 = f32[2560,4,8]{0,2,1:T(8,128)S(1)} fusion(f32[4,128,2560,8]{2,1,3,0:T(8,128)} %get-tuple-element.444, f32[2560,4,8]{0,2,1:T(8,128)S(1)} %max.17), kind=kLoop, calls=%fused_computation.32.clone.1 | loop fusion | flops 31375360 | bytes 42598400 | tf_op jit(solution)/shard_map/while/body/eval_jaxpr/reduce_sum | solution.py:24
  903.2 42.9 %bitcast_add_fusion.5 = f32[2560,4,8,128]{0,3,2,1:T(8,128)} fusion(f32[2560,4,8,128]{0,3,2,1:T(8,128)} %get-tuple-element.495, f32[4,128,2560,8]{2,1,3,0:T(8,128)} %get-tuple-element.444, f32[2560,4,8]{0,2,1:T(8,128)} %get-tuple-element.446, f32[2560,4,8]{0,2,1:T(8,128)S(1)} %max.17, bf16[1,128,4,128]{1,3,2,0:T(8,128)(2,1)} %copy-done.4), kind=kOutput, calls=%fused_computation.27.clone.1 | convolution fusion | flops 2736783360 | bytes 126615552 | tf_op jit(solution)/shard_map/while/body/eval_jaxpr/rhgk,khd->rhgd/dot_general | solution.py:25
  951.8 21.2 %bitcast_reduce_fusion.2 = (f32[2560,4,8]{0,2,1:T(8,128)}, f32[4,128,2560,8]{2,1,3,0:T(8,128)}) fusion(bf16[2560,4,8,128]{3,0,2,1:T(8,128)(2,1)} %get-tuple-element.515, bf16[1,128,4,128]{3,2,1,0:T(4,128)(2,1)S(1)} %get-tuple-element.437), kind=kOutput, calls=%fused_computation.29.clone.1 | convolution fusion | flops 2705244160 | bytes 63373312 | tf_op jit(solution)/shard_map/while/body/eval_jaxpr/rhgd,khd->rhgk/dot_general | solution.py:148
  974.2 17.1 %fusion.79 = f32[2560,4,8]{0,2,1:T(8,128)S(1)} fusion(f32[4,128,2560,8]{2,1,3,0:T(8,128)} %get-tuple-element.444, f32[2560,4,8]{0,2,1:T(8,128)S(1)} %max.17), kind=kLoop, calls=%fused_computation.32.clone.1 | loop fusion | flops 31375360 | bytes 42598400 | tf_op jit(solution)/shard_map/while/body/eval_jaxpr/reduce_sum | solution.py:24
  993.0 42.9 %bitcast_add_fusion.5 = f32[2560,4,8,128]{0,3,2,1:T(8,128)} fusion(f32[2560,4,8,128]{0,3,2,1:T(8,128)} %get-tuple-element.495, f32[4,128,2560,8]{2,1,3,0:T(8,128)} %get-tuple-element.444, f32[2560,4,8]{0,2,1:T(8,128)} %get-tuple-element.446, f32[2560,4,8]{0,2,1:T(8,128)S(1)} %max.17, bf16[1,128,4,128]{1,3,2,0:T(8,128)(2,1)} %copy-done.4), kind=kOutput, calls=%fused_computation.27.clone.1 | convolution fusion | flops 2736783360 | bytes 126615552 | tf_op jit(solution)/shard_map/while/body/eval_jaxpr/rhgk,khd->rhgd/dot_general | solution.py:25
  1041.6 21.2 %bitcast_reduce_fusion.2 = (f32[2560,4,8]{0,2,1:T(8,128)}, f32[4,128,2560,8]{2,1,3,0:T(8,128)}) fusion(bf16[2560,4,8,128]{3,0,2,1:T(8,128)(2,1)} %get-tuple-element.515, bf16[1,128,4,128]{3,2,1,0:T(4,128)(2,1)S(1)} %get-tuple-element.437), kind=kOutput, calls=%fused_computation.29.clone.1 | convolution fusion | flops 2705244160 | bytes 63373312 | tf_op jit(solution)/shard_map/while/body/eval_jaxpr/rhgd,khd->rhgk/dot_general | solution.py:148
  1064.0 17.1 %fusion.79 = f32[2560,4,8]{0,2,1:T(8,128)S(1)} fusion(f32[4,128,2560,8]{2,1,3,0:T(8,128)} %get-tuple-element.444, f32[2560,4,8]{0,2,1:T(8,128)S(1)} %max.17), kind=kLoop, calls=%fused_computation.32.clone.1 | loop fusion | flops 31375360 | bytes 42598400 | tf_op jit(solution)/shard_map/while/body/eval_jaxpr/reduce_sum | solution.py:24
  1082.7 42.9 %bitcast_add_fusion.5 = f32[2560,4,8,128]{0,3,2,1:T(8,128)} fusion(f32[2560,4,8,128]{0,3,2,1:T(8,128)} %get-tuple-element.495, f32[4,128,2560,8]{2,1,3,0:T(8,128)} %get-tuple-element.444, f32[2560,4,8]{0,2,1:T(8,128)} %get-tuple-element.446, f32[2560,4,8]{0,2,1:T(8,128)S(1)} %max.17, bf16[1,128,4,128]{1,3,2,0:T(8,128)(2,1)} %copy-done.4), kind=kOutput, calls=%fused_computation.27.clone.1 | convolution fusion | flops 2736783360 | bytes 126615552 | tf_op jit(solution)/shard_map/while/body/eval_jaxpr/rhgk,khd->rhgd/dot_general | solution.py:25
  1126.3 23.2 %divide_convert_fusion = bf16[2560,4,8,128]{0,3,2,1:T(8,128)(2,1)} fusion(f32[2560,4,8,128]{0,3,2,1:T(8,128)} %get-tuple-element.121, f32[2560,4,8]{0,2,1:T(8,128)} %get-tuple-element.122), kind=kLoop, calls=%fused_computation.68 | loop fusion | flops 20971520 | bytes 63242240 | tf_op jit(solution)/shard_map/convert_element_type | solution.py:58
  1149.5 28.1 %copy.101 = bf16[2560,4096]{1,0:T(8,128)(2,1)} copy(bf16[2560,4096]{0,1:T(8,128)(2,1)} %bitcast.162) | data formatting | bytes 41943040 | tf_op jit(solution)/shard_map/reshape | solution.py:58
  (273 shorter events, 221.5 us)
Async XLA Ops:
  7.2 204.4 %all-gather.3.cloned.1.call-start = ((), (), s32[]{:S(2)}) async-start(), calls=%async_computation | async-start | bytes 13107200 | tf_op jit(solution)/shard_map/all_gather | solution.py:87
  7.9 10.7 copy-start.15
  7.9 11.0 copy-start.13
  7.9 388.3 %all-gather.5.cloned.1.call-start = ((), (), s32[]{:S(2)}) async-start(), calls=%async_computation.1 | async-start | bytes 13107200 | tf_op jit(solution)/shard_map/all_gather | solution.py:88
  8.7 42.1 %copy-start.14 = (bf16[128,512]{1,0:T(8,128)(2,1)S(1)}, bf16[128,512]{1,0:T(8,128)(2,1)}, u32[]{:S(2)}) copy-start(bf16[128,512]{1,0:T(8,128)(2,1)} %param.13) | copy-start | bytes 393220
  8.7 66.1 %copy-start.11 = (bf16[128,4096]{1,0:T(8,128)(2,1)S(1)}, bf16[128,4096]{1,0:T(8,128)(2,1)}, u32[]{:S(2)}) copy-start(bf16[128,4096]{1,0:T(8,128)(2,1)} %param.11) | copy-start | bytes 3145732
  439.7 4.0 copy-start.5
  443.8 2.1 copy-start.8
  443.8 2.5 copy-start.9
  727.2 0.7 copy-start.2
  727.9 39.2 %copy-start = (f32[128,4,8,128]{0,3,2,1:T(8,128)S(1)}, f32[128,4,8,128]{0,3,2,1:T(8,128)}, u32[]{:S(2)}) copy-start(f32[128,4,8,128]{0,3,2,1:T(8,128)} %custom-call.2) | copy-start | bytes 6291460
  727.9 39.2 %copy-start.1 = (bf16[128,4,8,128]{3,0,2,1:T(8,128)(2,1)S(1)}, bf16[128,4,8,128]{3,0,2,1:T(8,128)(2,1)}, u32[]{:S(2)}) copy-start(bf16[128,4,8,128]{3,0,2,1:T(8,128)(2,1)} %copy.84) | copy-start | bytes 3145732
  728.0 39.2 %copy-start.10 = (f32[128,4,8]{0,2,1:T(8,128)S(1)}, f32[128,4,8]{0,2,1:T(8,128)}, u32[]{:S(2)}) copy-start(f32[128,4,8]{0,2,1:T(8,128)} %custom-call) | copy-start | bytes 49156
  728.0 39.2 %copy-start.12 = (f32[128,4,8]{0,2,1:T(8,128)S(1)}, f32[128,4,8]{0,2,1:T(8,128)}, u32[]{:S(2)}) copy-start(f32[128,4,8]{0,2,1:T(8,128)} %custom-call.1) | copy-start | bytes 49156
  770.1 23.4 %copy-start.4 = (bf16[1,128,4,128]{1,3,2,0:T(8,128)(2,1)}, bf16[1,128,4,128]{1,3,2,0:T(8,128)(2,1)S(1)}, u32[]{:S(2)}) copy-start(bf16[1,128,4,128]{1,3,2,0:T(8,128)(2,1)S(1)} %copy.134) | copy-start | bytes 393220 | tf_op jit(solution)/shard_map/while
  794.6 17.1 %copy-start.3 = (f32[2560,4,8]{0,2,1:T(8,128)S(1)}, f32[2560,4,8]{0,2,1:T(8,128)}, u32[]{:S(2)}) copy-start(f32[2560,4,8]{0,2,1:T(8,128)} %get-tuple-element.493) | copy-start | bytes 983044 | tf_op jit(solution)/shard_map/while
  794.6 17.1 %copy-start.6 = (f32[2560,4,8]{0,2,1:T(8,128)S(1)}, f32[2560,4,8]{0,2,1:T(8,128)}, u32[]{:S(2)}) copy-start(f32[2560,4,8]{0,2,1:T(8,128)} %get-tuple-element.494) | copy-start | bytes 983044 | tf_op jit(solution)/shard_map/while
  812.7 0.7 copy-start.7
  859.8 23.4 %copy-start.4 = (bf16[1,128,4,128]{1,3,2,0:T(8,128)(2,1)}, bf16[1,128,4,128]{1,3,2,0:T(8,128)(2,1)S(1)}, u32[]{:S(2)}) copy-start(bf16[1,128,4,128]{1,3,2,0:T(8,128)(2,1)S(1)} %copy.134) | copy-start | bytes 393220 | tf_op jit(solution)/shard_map/while
  884.4 17.1 %copy-start.3 = (f32[2560,4,8]{0,2,1:T(8,128)S(1)}, f32[2560,4,8]{0,2,1:T(8,128)}, u32[]{:S(2)}) copy-start(f32[2560,4,8]{0,2,1:T(8,128)} %get-tuple-element.493) | copy-start | bytes 983044 | tf_op jit(solution)/shard_map/while
  884.4 17.1 %copy-start.6 = (f32[2560,4,8]{0,2,1:T(8,128)S(1)}, f32[2560,4,8]{0,2,1:T(8,128)}, u32[]{:S(2)}) copy-start(f32[2560,4,8]{0,2,1:T(8,128)} %get-tuple-element.494) | copy-start | bytes 983044 | tf_op jit(solution)/shard_map/while
  902.4 0.7 copy-start.7
  949.6 23.4 %copy-start.4 = (bf16[1,128,4,128]{1,3,2,0:T(8,128)(2,1)}, bf16[1,128,4,128]{1,3,2,0:T(8,128)(2,1)S(1)}, u32[]{:S(2)}) copy-start(bf16[1,128,4,128]{1,3,2,0:T(8,128)(2,1)S(1)} %copy.134) | copy-start | bytes 393220 | tf_op jit(solution)/shard_map/while
  974.2 17.1 %copy-start.3 = (f32[2560,4,8]{0,2,1:T(8,128)S(1)}, f32[2560,4,8]{0,2,1:T(8,128)}, u32[]{:S(2)}) copy-start(f32[2560,4,8]{0,2,1:T(8,128)} %get-tuple-element.493) | copy-start | bytes 983044 | tf_op jit(solution)/shard_map/while
  974.2 17.1 %copy-start.6 = (f32[2560,4,8]{0,2,1:T(8,128)S(1)}, f32[2560,4,8]{0,2,1:T(8,128)}, u32[]{:S(2)}) copy-start(f32[2560,4,8]{0,2,1:T(8,128)} %get-tuple-element.494) | copy-start | bytes 983044 | tf_op jit(solution)/shard_map/while
  992.2 0.7 copy-start.7
  1039.4 23.4 %copy-start.4 = (bf16[1,128,4,128]{1,3,2,0:T(8,128)(2,1)}, bf16[1,128,4,128]{1,3,2,0:T(8,128)(2,1)S(1)}, u32[]{:S(2)}) copy-start(bf16[1,128,4,128]{1,3,2,0:T(8,128)(2,1)S(1)} %copy.134) | copy-start | bytes 393220 | tf_op jit(solution)/shard_map/while
  1063.9 17.1 %copy-start.3 = (f32[2560,4,8]{0,2,1:T(8,128)S(1)}, f32[2560,4,8]{0,2,1:T(8,128)}, u32[]{:S(2)}) copy-start(f32[2560,4,8]{0,2,1:T(8,128)} %get-tuple-element.493) | copy-start | bytes 983044 | tf_op jit(solution)/shard_map/while
  1063.9 17.1 %copy-start.6 = (f32[2560,4,8]{0,2,1:T(8,128)S(1)}, f32[2560,4,8]{0,2,1:T(8,128)}, u32[]{:S(2)}) copy-start(f32[2560,4,8]{0,2,1:T(8,128)} %get-tuple-element.494) | copy-start | bytes 983044 | tf_op jit(solution)/shard_map/while
  1082.0 0.7 copy-start.7
Sparse Core Ops, SparseCore 0:
  9.6 201.9 all-gather.2
  213.1 183.0 all-gather.4
where the time goes:
time: 1190 us
  matrix products  390 us (33%)
  local copies, waits for them, and re-layouts  372 us (31%)
  waiting for transfers between devices  214 us (18%)
  other arithmetic  140 us (12%)
  blocking collectives  54.1 us (5%)
  between operations  14.2 us (1%)
    dot_general x8, matrix products, absorb(): jnp.einsum('rhgk,khd->rhgd', weights.astype(jnp.bfloat16), value_rows, pr...  176 us
    all_gather x1, waiting for transfers between devices, local(): lax.all_gather(tree_value_array, 'ctx', axis=0, tiled=True)  158 us
    unnamed x30, local copies, waits for them, and re-layouts  114 us
    dynamic_update_slice x60, local copies, waits for them, and re-layouts, local(): lax.map(local_part, (tree_queries, all_keys, all_values, allowed))  89.8 us
    dot_general x4, matrix products, scan_step(): jnp.einsum('rhgd,khd->rhgk', flat_queries, block_keys, preferred_element_...  84.9 us
    dot_general x20, matrix products, local_part(): jnp.einsum('rhgk,khd->rhgd', weights.astype(jnp.bfloat16), value_rows, pr...  79.6 us
    reduce_sum x8, other arithmetic, absorb(): totals = totals * factor + jnp.sum(weights, axis=-1)  70.5 us
    all_gather x1, waiting for transfers between devices, local(): lax.all_gather(tree_key_array, 'ctx', axis=0, tiled=True)  55.1 us
  transfers between devices with their start and end apart: 2, of which 2 were waited for; matrix products, arithmetic and copies ran while one was open for 10% of the time, Pallas kernels for 0%

commit v1 on v0

v1 whole, which is shorter than its diff:
```python
import functools
import math

import jax
import jax.numpy as jnp
from jax import lax
from jax.experimental import pallas as pl
from jax.experimental.pallas import tpu as pltpu
from jax.sharding import PartitionSpec as P

HEAD_SIZE = 128
SEGMENT_TOKENS = 128
GROUP = 8
ROW_HEADS = 2
STAT_HALF = 64
MASKED = -1e30
LOG2E_SCALE = math.log2(math.e) / math.sqrt(HEAD_SIZE)


def stack_heads(ref, first, count):
    blocks = [
        ref[:, (first + h) * HEAD_SIZE : (first + h + 1) * HEAD_SIZE] for h in range(count)
    ]
    return jnp.concatenate(blocks, axis=0)


def scores_of(queries, key_rows):
    return lax.dot_general(
        queries, key_rows, (((1,), (1,)), ((), ())), preferred_element_type=jnp.float32
    )


def with_ones(value_rows):
    return jnp.concatenate([value_rows, jnp.ones_like(value_rows)], axis=1)


def head_cols(ref, j):
    return ref[:, j * HEAD_SIZE : (j + 1) * HEAD_SIZE]


def near_kernel(kv_heads, q_ref, kt_ref, vt_ref, ks_ref, vs_ref, o_ref, stat_ref):
    rows = ROW_HEADS * SEGMENT_TOKENS
    lane = lax.broadcasted_iota(jnp.int32, (SEGMENT_TOKENS, 2 * STAT_HALF), 1)
    query_at = lax.broadcasted_iota(jnp.int32, (rows, SEGMENT_TOKENS), 0) % SEGMENT_TOKENS
    key_at = lax.broadcasted_iota(jnp.int32, (rows, SEGMENT_TOKENS), 1)
    causal = query_at >= key_at
    stats = jnp.zeros((SEGMENT_TOKENS, 2 * STAT_HALF), jnp.float32)
    for j in range(kv_heads):
        trunk_keys, self_keys = head_cols(kt_ref, j), head_cols(ks_ref, j)
        trunk_values = with_ones(head_cols(vt_ref, j))
        self_values = with_ones(head_cols(vs_ref, j))
        for first in range(j * GROUP, (j + 1) * GROUP, ROW_HEADS):
            queries = stack_heads(q_ref, first, ROW_HEADS)
            trunk_scores = scores_of(queries, trunk_keys)
            self_scores = jnp.where(causal, scores_of(queries, self_keys), MASKED)
            peak = jnp.maximum(
                jnp.max(trunk_scores, axis=1, keepdims=True),
                jnp.max(self_scores, axis=1, keepdims=True),
            )
            trunk_weights = jnp.exp2((trunk_scores - peak) * LOG2E_SCALE).astype(jnp.bfloat16)
            self_weights = jnp.exp2((self_scores - peak) * LOG2E_SCALE).astype(jnp.bfloat16)
            summed = jnp.dot(
                trunk_weights, trunk_values, preferred_element_type=jnp.float32
            ) + jnp.dot(self_weights, self_values, preferred_element_type=jnp.float32)
            for h in range(ROW_HEADS):
                part = slice(h * SEGMENT_TOKENS, (h + 1) * SEGMENT_TOKENS)
                head = first + h
                o_ref[:, head * HEAD_SIZE : (head + 1) * HEAD_SIZE] = summed[
                    part, :HEAD_SIZE
                ].astype(jnp.bfloat16)
                stats = jnp.where(lane == head, peak[part], stats)
                stats = jnp.where(lane == STAT_HALF + head, summed[part, HEAD_SIZE:], stats)
    stat_ref[...] = stats


def far_kernel(
    kv_heads, place_ref, seen_ref, q_ref, near_ref, stat_ref, kv0_ref, kv1_ref, o_ref
):
    step = pl.program_id(0)
    rows = ROW_HEADS * SEGMENT_TOKENS
    bars = [
        jnp.where(seen_ref[2 * step + n] > 0, 0.0, MASKED).astype(jnp.float32) for n in range(2)
    ]
    key_at = lax.broadcasted_iota(jnp.int32, (1, 2 * SEGMENT_TOKENS), 1)
    bar = jnp.where(key_at < SEGMENT_TOKENS, bars[0], bars[1])
    width = kv_heads * HEAD_SIZE
    for j in range(kv_heads):
        cols = slice(j * HEAD_SIZE, (j + 1) * HEAD_SIZE)
        vcols = slice(width + j * HEAD_SIZE, width + (j + 1) * HEAD_SIZE)
        keys = jnp.concatenate([kv0_ref[0, :, cols], kv1_ref[0, :, cols]], axis=0)
        values = with_ones(jnp.concatenate([kv0_ref[0, :, vcols], kv1_ref[0, :, vcols]], axis=0))
        for first in range(j * GROUP, (j + 1) * GROUP, ROW_HEADS):
            queries = stack_heads(q_ref, first, ROW_HEADS)
            scores = scores_of(queries, keys) + bar
            near_peak = jnp.concatenate(
                [stat_ref[:, first + h : first + h + 1] for h in range(ROW_HEADS)], axis=0
            )
            near_total = jnp.concatenate(
                [
                    stat_ref[:, STAT_HALF + first + h : STAT_HALF + first + h + 1]
                    for h in range(ROW_HEADS)
                ],
                axis=0,
            )
            peak = jnp.maximum(near_peak, jnp.max(scores, axis=1, keepdims=True))
            weights = jnp.exp2((scores - peak) * LOG2E_SCALE).astype(jnp.bfloat16)
            summed = jnp.dot(weights, values, preferred_element_type=jnp.float32)
            factor = jnp.exp2((near_peak - peak) * LOG2E_SCALE)
            near = stack_heads(near_ref, first, ROW_HEADS).astype(jnp.float32)
            total = factor * near_total + summed[:, HEAD_SIZE:]
            out = ((factor * near + summed[:, :HEAD_SIZE]) / total).astype(jnp.bfloat16)
            for h in range(ROW_HEADS):
                part = slice(h * SEGMENT_TOKENS, (h + 1) * SEGMENT_TOKENS)
                head = first + h
                o_ref[:, head * HEAD_SIZE : (head + 1) * HEAD_SIZE] = out[part]


def trunk_kernel(kv_heads, start_ref, q_ref, kt_ref, vt_ref, o_ref):
    rows = q_ref.shape[0]
    key_count = kt_ref.shape[0]
    query_at = start_ref[0] + lax.broadcasted_iota(jnp.int32, (rows, key_count), 0)
    causal = query_at >= lax.broadcasted_iota(jnp.int32, (rows, key_count), 1)
    for j in range(kv_heads):
        keys = head_cols(kt_ref, j)
        values = with_ones(head_cols(vt_ref, j))
        for head in range(j * GROUP, (j + 1) * GROUP):
            scores = jnp.where(causal, scores_of(head_cols(q_ref, head), keys), MASKED)
            peak = jnp.max(scores, axis=1, keepdims=True)
            weights = jnp.exp2((scores - peak) * LOG2E_SCALE).astype(jnp.bfloat16)
            summed = jnp.dot(weights, values, preferred_element_type=jnp.float32)
            o_ref[:, head * HEAD_SIZE : (head + 1) * HEAD_SIZE] = (
                summed[:, :HEAD_SIZE] / summed[:, HEAD_SIZE:]
            ).astype(jnp.bfloat16)


VMEM_LIMIT = 48 * 1024 * 1024


def near_call(tree_query, key_all, value_all, tree_key, tree_value):
    tokens, width = tree_query.shape
    slots = tokens // SEGMENT_TOKENS
    kv_width = tree_key.shape[1]
    kv_heads = kv_width // HEAD_SIZE
    trunk = key_all.shape[0]
    keys = trunk + SEGMENT_TOKENS
    whole = pl.BlockSpec((trunk, kv_width), lambda s: (0, 0))
    own = pl.BlockSpec((SEGMENT_TOKENS, kv_width), lambda s: (s, 0))
    wide = pl.BlockSpec((SEGMENT_TOKENS, width), lambda s: (s, 0))
    return pl.pallas_call(
        functools.partial(near_kernel, kv_heads),
        grid=(slots,),
        in_specs=[wide, whole, whole, own, own],
        out_specs=[wide, pl.BlockSpec((SEGMENT_TOKENS, 2 * STAT_HALF), lambda s: (s, 0))],
        out_shape=[
            jax.ShapeDtypeStruct((tokens, width), jnp.bfloat16),
            jax.ShapeDtypeStruct((tokens, 2 * STAT_HALF), jnp.float32),
        ],
        compiler_params=pltpu.CompilerParams(vmem_limit_bytes=VMEM_LIMIT),
        cost_estimate=pl.CostEstimate(
            flops=4 * tokens * width * keys,
            bytes_accessed=4 * tokens * width,
            transcendentals=tokens * width // HEAD_SIZE * keys,
        ),
        name="near",
    )(tree_query, key_all, value_all, tree_key, tree_value)


def far_call(places, seen, tree_query, near, stats, gathered):
    tokens, width = tree_query.shape
    slots = tokens // SEGMENT_TOKENS
    kv_width = gathered.shape[2]
    kv_heads = kv_width // HEAD_SIZE // 2
    wide = pl.BlockSpec((SEGMENT_TOKENS, width), lambda s, p, v: (s, 0))
    return pl.pallas_call(
        functools.partial(far_kernel, kv_heads),
        grid_spec=pltpu.PrefetchScalarGridSpec(
            num_scalar_prefetch=2,
            grid=(slots,),
            in_specs=[
                wide,
                wide,
                pl.BlockSpec((SEGMENT_TOKENS, 2 * STAT_HALF), lambda s, p, v: (s, 0)),
                pl.BlockSpec((1, SEGMENT_TOKENS, kv_width), lambda s, p, v: (p[2 * s], 0, 0)),
                pl.BlockSpec((1, SEGMENT_TOKENS, kv_width), lambda s, p, v: (p[2 * s + 1], 0, 0)),
            ],
            out_specs=wide,
        ),
        out_shape=jax.ShapeDtypeStruct((tokens, width), jnp.bfloat16),
        compiler_params=pltpu.CompilerParams(vmem_limit_bytes=VMEM_LIMIT),
        cost_estimate=pl.CostEstimate(
            flops=8 * tokens * width * SEGMENT_TOKENS,
            bytes_accessed=6 * tokens * width,
            transcendentals=tokens * width * 2,
        ),
        name="far",
    )(places, seen, tree_query, near, stats, gathered, gathered)


def trunk_call(start, trunk_query, key_all, value_all):
    rows, width = trunk_query.shape
    kv_heads = key_all.shape[1] // HEAD_SIZE
    vmem = pl.BlockSpec(memory_space=pltpu.VMEM)
    return pl.pallas_call(
        functools.partial(trunk_kernel, kv_heads),
        in_specs=[pl.BlockSpec(memory_space=pltpu.SMEM), vmem, vmem, vmem],
        out_specs=vmem,
        out_shape=jax.ShapeDtypeStruct((rows, width), jnp.bfloat16),
        compiler_params=pltpu.CompilerParams(vmem_limit_bytes=VMEM_LIMIT),
        cost_estimate=pl.CostEstimate(
            flops=4 * rows * width * key_all.shape[0],
            bytes_accessed=4 * rows * width,
            transcendentals=rows * width // HEAD_SIZE * key_all.shape[0],
        ),
        name="trunk",
    )(start, trunk_query, key_all, value_all)


def local(
    trunk_query,
    trunk_key,
    trunk_value,
    tree_query,
    tree_key,
    tree_value,
    ancestors,
):
    me = lax.axis_index("ctx")
    kv_width = trunk_key.shape[1]
    slots = tree_query.shape[0] // SEGMENT_TOKENS
    total = ancestors.shape[0]
    sent = slots * 4 // 5

    slot_ids = jnp.arange(total, dtype=jnp.int32)
    inner = jnp.any(ancestors.reshape(-1, 1) == slot_ids[None, :], axis=0)
    earlier = (slot_ids[None, :] < slot_ids[:, None]) & (
        slot_ids[None, :] // slots == slot_ids[:, None] // slots
    )
    rank = jnp.sum(jnp.where(earlier & inner[None, :], 1, 0), axis=1)
    place = slot_ids // slots * sent + rank
    own_place = me * sent + jnp.arange(sent, dtype=jnp.int32)
    hit = inner[None, :] & (place[None, :] == own_place[:, None])
    picked = jnp.sum(jnp.where(hit, slot_ids[None, :] % slots, 0), axis=1)

    own_lists = lax.dynamic_slice_in_dim(ancestors, me * slots, slots, 0).reshape(-1)
    seen = (own_lists >= 0).astype(jnp.int32)
    places = jnp.sum(
        jnp.where(own_lists[:, None] == slot_ids[None, :], place[None, :], 0), axis=1
    )

    trunk_both = lax.all_gather(
        jnp.concatenate([trunk_key, trunk_value], axis=1), "ctx", axis=0, tiled=True
    )
    key_all, value_all = trunk_both[:, :kv_width], trunk_both[:, kv_width:]
    packed = jnp.concatenate(
        [
            tree_key.reshape(slots, SEGMENT_TOKENS, kv_width)[picked],
            tree_value.reshape(slots, SEGMENT_TOKENS, kv_width)[picked],
        ],
        axis=2,
    )
    gathered = lax.all_gather(packed, "ctx", axis=0, tiled=True)

    near, stats = near_call(tree_query, key_all, value_all, tree_key, tree_value)
    start = (me * trunk_query.shape[0]).astype(jnp.int32).reshape(1)
    trunk_out = trunk_call(start, trunk_query, key_all, value_all)
    tree_out = far_call(places, seen, tree_query, near, stats, gathered)
    return trunk_out, tree_out


def solution(mesh):
    split = P(("rep", "ctx"), "head")
    return jax.shard_map(
        local,
        mesh=mesh,
        in_specs=(split,) * 6 + (P("rep", None),),
        out_specs=(split, split),
        check_vma=False,
    )
```

time: 1190 us -> 451 us (0.38)
  matrix products: 390 us -> 0 us
  local copies, waits for them, and re-layouts: 372 us -> 12.4 us
  Pallas kernels: 0 us -> 216 us
  other arithmetic: 140 us -> 7.38 us
  blocking collectives: 54.1 us -> 0 us
  waiting for transfers between devices: 214 us -> 200 us
    dot_general x56 -> x0, matrix products: 390 us -> none  [the longest x8 176 us: absorb(): jnp.einsum('rhgk,khd->rhgd', weights.astype(jnp.bfloat16), value_rows, pr...]
    pallas_call x0 -> x3, Pallas kernels: none -> 216 us  [the longest x1 113 us: far_call(): pl.pallas_call(functools.partial(far_kernel, kv_heads), grid_spec=pltpu.P...]
    unnamed x30 -> x11, local copies, waits for them, and re-layouts: 114 us -> 5.04 us
    reshape x12 -> x0, local copies, waits for them, and re-layouts: 102 us -> none  [the longest x2 29.4 us: finish(): (weighted / totals[..., None]).astype(jnp.bfloat16)]
    reduce_sum x28 -> x3, other arithmetic: 102 us -> 0.54 us  [the longest x1 0.18 us: local(): picked = jnp.sum(jnp.where(hit, slot_ids[None, :] % slots, 0), axis=1)]
    dynamic_update_slice x60 -> x0, local copies, waits for them, and re-layouts: 89.8 us -> none  [local(): lax.map(local_part, (tree_queries, all_keys, all_values, allowed))]
    all_gather x2 -> x0, blocking collectives: 54.1 us -> none  [the longest x1 30.9 us: local(): key_piece = lax.all_gather(trunk_key_array, 'ctx', axis=0, tiled=True)]
    dynamic_slice x28 -> x2, local copies, waits for them, and re-layouts: 36.8 us -> 0.17 us  [local(): lax.dynamic_slice_in_dim(ancestors, me * slots, slots, 0).reshape(-1)]
  transfers between devices with their start and end apart: 2 -> 2, of which waited for: 2 -> 2; matrix products, arithmetic and copies ran while one was open for 10% -> 3% of each run, Pallas kernels for 0% -> 23%
where the time goes in v1:
time: 451 us
  Pallas kernels  216 us (48%)
  waiting for transfers between devices  200 us (44%)
  between operations  14.1 us (3%)
  local copies, waits for them, and re-layouts  12.4 us (3%)
  other arithmetic  7.38 us (2%)
    all_gather x1, waiting for transfers between devices, local(): gathered = lax.all_gather(packed, 'ctx', axis=0, tiled=True)  182 us
    pallas_call x1, Pallas kernels, far_call(): pl.pallas_call(functools.partial(far_kernel, kv_heads), grid_spec=pltpu.P...  113 us
    pallas_call x1, Pallas kernels, near_call(): pl.pallas_call(functools.partial(near_kernel, kv_heads), grid=(slots,), i...  99.5 us
    all_gather x1, waiting for transfers between devices, local(): lax.all_gather(jnp.concatenate([trunk_key, trunk_value], axis=1), 'ctx',...  18.5 us
  transfers between devices with their start and end apart: 2, of which 2 were waited for; matrix products, arithmetic and copies ran while one was open for 3% of the time, Pallas kernels for 23%

profile of v1, /device:TPU:0, one launch (start us, length us, event | category | flops | bytes accessed | tf_op | source)
XLA Modules:
  0.0 450.5 jit_solution(18431806217890626659)
XLA Ops:
  7.2 0.0 copy-start
  7.2 0.0 all-gather.3.cloned.1.call-start
  7.2 1.8 pad_maximum_fusion.1
  9.1 0.0 all-gather.3.cloned.1.call-update
  9.1 0.0 all-gather.5.cloned.1.call-start
  9.1 0.8 copy.15
  9.9 0.1 eq.65
  10.1 0.1 fusion
  10.2 0.2 select_reduce_fusion
  10.4 0.2 select_reduce_fusion.2
  10.6 3.8 gather_fusion.1
  14.4 0.0 copy-done
  14.4 2.0 gather_fusion
  16.4 4.8 %pad_maximum_fusion = bf16[16,128,1024]{2,1,0:T(8,128)(2,1)} fusion(bf16[16,128,512]{2,1,0:T(8,128)(2,1)} %gather_fusion.1, bf16[16,128,512]{2,1,0:T(8,128)(2,1)} %gather_fusion), kind=kLoop, calls=%fused_computation.2 | loop fusion | flops 8388608 | bytes 8388608 | tf_op jit(solution)/shard_map/concatenate | solution.py:254
  21.2 0.0 copy-start.4
  21.2 0.0 all-gather.5.cloned.1.call-update
  21.2 0.6 copy-done.4
  21.9 0.1 constant_dynamic-slice_fusion
  21.9 0.1 copy.14
  22.0 0.1 eq.58
  22.1 0.2 select_reduce_fusion.1.place_ref
  22.3 18.5 %all-gather.3.cloned.1.call-done = bf16[512,1024]{1,0:T(8,128)(2,1)} async-done(((bf16[128,1024]{1,0:T(8,128)(2,1)}), bf16[512,1024]{1,0:T(8,128)(2,1)}) %all-gather.3.cloned.1.call-update) | async-done | bytes 1048592 | tf_op jit(solution)/shard_map/all_gather | solution.py:250
  40.8 1.3 fusion.4
  42.1 0.0 copy-start.3
  42.1 1.2 copy-done.3
  43.3 3.7 trunk.1
  47.0 99.5 %near.1 = (bf16[2560,4096]{1,0:T(8,128)(2,1)}, f32[2560,128]{1,0:T(8,128)S(1)}) custom-call(bf16[2560,4096]{1,0:T(8,128)(2,1)} %q_ref.5, bf16[512,512]{1,0:T(8,128)(2,1)S(1)} %get-tuple-element.7.kt_ref, bf16[512,512]{1,0:T(8,128)(2,1)S(1)} %get-tuple-element.6.vt_ref, bf16[2560,512]{1,0:T(8,128)(2,1)S(1)} %copy-done, bf16[2560,512]{1,0:T(8,128)(2,1)} %vs_ref.1), custom_call_target="tpu_custom_call" | custom-call | flops 26843545600 | bytes 41943040 | tf_op jit(solution)/shard_map/near/pallas_call | solution.py:149
  146.6 0.0 copy-start.1
  146.6 1.1 copy-done.1
  147.6 181.6 %all-gather.5.cloned.1.call-done.kv0_ref.kv1_ref = bf16[64,128,1024]{2,1,0:T(8,128)(2,1)} async-done(((bf16[16,128,1024]{2,1,0:T(8,128)(2,1)}), bf16[64,128,1024]{2,1,0:T(8,128)(2,1)}) %all-gather.5.cloned.1.call-update) | async-done | bytes 16777232 | tf_op jit(solution)/shard_map/all_gather | solution.py:261
  329.3 0.0 copy-start.2
  329.3 1.3 copy-done.2
  330.6 113.1 %far.1 = bf16[2560,4096]{1,0:T(8,128)(2,1)} custom-call(s32[40]{0:T(128)S(1)} %select_reduce_fusion.1.place_ref, s32[40]{0:T(128)S(1)} %compare_convert_fusion.seen_ref, bf16[2560,4096]{1,0:T(8,128)(2,1)} %q_ref.5, bf16[2560,4096]{1,0:T(8,128)(2,1)} %get-tuple-element.4.near_ref, f32[2560,128]{1,0:T(8,128)S(1)} %copy-done.2, ...), custom_call_target="tpu_custom_call" | custom-call | flops 10737418240 | bytes 62914560 | tf_op jit(solution)/shard_map/far/pallas_call | solution.py:174
  (6 shorter events, 0.0 us)
Async XLA Ops:
  7.2 7.2 %copy-start = (bf16[2560,512]{1,0:T(8,128)(2,1)S(1)}, bf16[2560,512]{1,0:T(8,128)(2,1)}, u32[]{:S(2)}) copy-start(bf16[2560,512]{1,0:T(8,128)(2,1)} %ks_ref.1) | copy-start | bytes 7864324
  7.2 33.6 %all-gather.3.cloned.1.call-start = ((), (), s32[]{:S(2)}) async-start(), calls=%async_computation | async-start | bytes 1310720 | tf_op jit(solution)/shard_map/all_gather | solution.py:250
  9.1 320.2 %all-gather.5.cloned.1.call-start = ((), (), s32[]{:S(2)}) async-start(), calls=%async_computation.1 | async-start | bytes 20971520 | tf_op jit(solution)/shard_map/all_gather | solution.py:261
  21.2 0.7 copy-start.4
  42.1 1.2 copy-start.3
  146.6 1.1 copy-start.1
  329.3 1.3 copy-start.2
Sparse Core Ops, SparseCore 0:
  10.2 30.6 all-gather.2
  43.0 286.2 all-gather.4

commit v2 on v1

--- a/solution.py
+++ b/solution.py
@@ -12,7 +12,7 @@
 SEGMENT_TOKENS = 128
 GROUP = 8
 ROW_HEADS = 2
-STAT_HALF = 64
+STAT_WIDTH = 128
 MASKED = -1e30
 LOG2E_SCALE = math.log2(math.e) / math.sqrt(HEAD_SIZE)
 
@@ -40,11 +40,11 @@
 
 def near_kernel(kv_heads, q_ref, kt_ref, vt_ref, ks_ref, vs_ref, o_ref, stat_ref):
     rows = ROW_HEADS * SEGMENT_TOKENS
-    lane = lax.broadcasted_iota(jnp.int32, (SEGMENT_TOKENS, 2 * STAT_HALF), 1)
+    lane = lax.broadcasted_iota(jnp.int32, (SEGMENT_TOKENS, STAT_WIDTH), 1)
     query_at = lax.broadcasted_iota(jnp.int32, (rows, SEGMENT_TOKENS), 0) % SEGMENT_TOKENS
     key_at = lax.broadcasted_iota(jnp.int32, (rows, SEGMENT_TOKENS), 1)
     causal = query_at >= key_at
-    stats = jnp.zeros((SEGMENT_TOKENS, 2 * STAT_HALF), jnp.float32)
+    stats = jnp.zeros((SEGMENT_TOKENS, STAT_WIDTH), jnp.float32)
     for j in range(kv_heads):
         trunk_keys, self_keys = head_cols(kt_ref, j), head_cols(ks_ref, j)
         trunk_values = with_ones(head_cols(vt_ref, j))
@@ -65,49 +65,53 @@
             for h in range(ROW_HEADS):
                 part = slice(h * SEGMENT_TOKENS, (h + 1) * SEGMENT_TOKENS)
                 head = first + h
-                o_ref[:, head * HEAD_SIZE : (head + 1) * HEAD_SIZE] = summed[
-                    part, :HEAD_SIZE
-                ].astype(jnp.bfloat16)
-                stats = jnp.where(lane == head, peak[part], stats)
-                stats = jnp.where(lane == STAT_HALF + head, summed[part, HEAD_SIZE:], stats)
+                total = summed[part, HEAD_SIZE:]
+                o_ref[:, head * HEAD_SIZE : (head + 1) * HEAD_SIZE] = (
+                    summed[part, :HEAD_SIZE] / total
+                ).astype(jnp.bfloat16)
+                level = peak[part] * LOG2E_SCALE + jnp.log2(total)
+                stats = jnp.where(lane == head, level, stats)
     stat_ref[...] = stats
 
 
 def far_kernel(
-    kv_heads, place_ref, seen_ref, q_ref, near_ref, stat_ref, kv0_ref, kv1_ref, o_ref
+    first_kv,
+    kv_count,
+    place_ref,
+    seen_ref,
+    q_ref,
+    near_ref,
+    stat_ref,
+    kv0_ref,
+    kv1_ref,
+    *rest,
 ):
+    o_ref = rest[-1]
     step = pl.program_id(0)
-    rows = ROW_HEADS * SEGMENT_TOKENS
     bars = [
         jnp.where(seen_ref[2 * step + n] > 0, 0.0, MASKED).astype(jnp.float32) for n in range(2)
     ]
     key_at = lax.broadcasted_iota(jnp.int32, (1, 2 * SEGMENT_TOKENS), 1)
     bar = jnp.where(key_at < SEGMENT_TOKENS, bars[0], bars[1])
-    width = kv_heads * HEAD_SIZE
-    for j in range(kv_heads):
+    width = kv_count * HEAD_SIZE
+    for j in range(kv_count):
         cols = slice(j * HEAD_SIZE, (j + 1) * HEAD_SIZE)
         vcols = slice(width + j * HEAD_SIZE, width + (j + 1) * HEAD_SIZE)
         keys = jnp.concatenate([kv0_ref[0, :, cols], kv1_ref[0, :, cols]], axis=0)
         values = with_ones(jnp.concatenate([kv0_ref[0, :, vcols], kv1_ref[0, :, vcols]], axis=0))
         for first in range(j * GROUP, (j + 1) * GROUP, ROW_HEADS):
             queries = stack_heads(q_ref, first, ROW_HEADS)
-            scores = scores_of(queries, keys) + bar
-            near_peak = jnp.concatenate(
-                [stat_ref[:, first + h : first + h + 1] for h in range(ROW_HEADS)], axis=0
+            scores = scores_of(queries, keys) * LOG2E_SCALE + bar
+            stat = first_kv * GROUP + first
+            level = jnp.concatenate(
+                [stat_ref[:, stat + h : stat + h + 1] for h in range(ROW_HEADS)], axis=0
             )
-            near_total = jnp.concatenate(
-                [
-                    stat_ref[:, STAT_HALF + first + h : STAT_HALF + first + h + 1]
-                    for h in range(ROW_HEADS)
-                ],
-                axis=0,
-            )
-            peak = jnp.maximum(near_peak, jnp.max(scores, axis=1, keepdims=True))
-            weights = jnp.exp2((scores - peak) * LOG2E_SCALE).astype(jnp.bfloat16)
+            peak = jnp.maximum(level, jnp.max(scores, axis=1, keepdims=True))
+            weights = jnp.exp2(scores - peak).astype(jnp.bfloat16)
             summed = jnp.dot(weights, values, preferred_element_type=jnp.float32)
-            factor = jnp.exp2((near_peak - peak) * LOG2E_SCALE)
+            factor = jnp.exp2(level - peak)
             near = stack_heads(near_ref, first, ROW_HEADS).astype(jnp.float32)
-            total = factor * near_total + summed[:, HEAD_SIZE:]
+            total = factor + summed[:, HEAD_SIZE:]
             out = ((factor * near + summed[:, :HEAD_SIZE]) / total).astype(jnp.bfloat16)
             for h in range(ROW_HEADS):
                 part = slice(h * SEGMENT_TOKENS, (h + 1) * SEGMENT_TOKENS)
@@ -150,10 +154,10 @@
         functools.partial(near_kernel, kv_heads),
         grid=(slots,),
         in_specs=[wide, whole, whole, own, own],
-        out_specs=[wide, pl.BlockSpec((SEGMENT_TOKENS, 2 * STAT_HALF), lambda s: (s, 0))],
+        out_specs=[wide, pl.BlockSpec((SEGMENT_TOKENS, STAT_WIDTH), lambda s: (s, 0))],
         out_shape=[
             jax.ShapeDtypeStruct((tokens, width), jnp.bfloat16),
-            jax.ShapeDtypeStruct((tokens, 2 * STAT_HALF), jnp.float32),
+            jax.ShapeDtypeStruct((tokens, STAT_WIDTH), jnp.float32),
         ],
         compiler_params=pltpu.CompilerParams(vmem_limit_bytes=VMEM_LIMIT),
         cost_estimate=pl.CostEstimate(
@@ -165,35 +169,42 @@
     )(tree_query, key_all, value_all, tree_key, tree_value)
 
 
-def far_call(places, seen, tree_query, near, stats, gathered):
+def far_call(places, seen, tree_query, near, stats, gathered, first_kv, earlier):
     tokens, width = tree_query.shape
     slots = tokens // SEGMENT_TOKENS
     kv_width = gathered.shape[2]
-    kv_heads = kv_width // HEAD_SIZE // 2
-    wide = pl.BlockSpec((SEGMENT_TOKENS, width), lambda s, p, v: (s, 0))
+    kv_count = kv_width // HEAD_SIZE // 2
+    share = kv_count * GROUP * HEAD_SIZE
+    column = first_kv // kv_count
+    wide = pl.BlockSpec((SEGMENT_TOKENS, share), lambda s, p, v: (s, column))
+    in_specs = [
+        wide,
+        wide,
+        pl.BlockSpec((SEGMENT_TOKENS, STAT_WIDTH), lambda s, p, v: (s, 0)),
+        pl.BlockSpec((1, SEGMENT_TOKENS, kv_width), lambda s, p, v: (p[2 * s], 0, 0)),
+        pl.BlockSpec((1, SEGMENT_TOKENS, kv_width), lambda s, p, v: (p[2 * s + 1], 0, 0)),
+    ]
+    operands = [places, seen, tree_query, near, stats, gathered, gathered]
+    aliases = {}
+    if earlier is not None:
+        aliases = {len(operands): 0}
+        in_specs.append(pl.BlockSpec(memory_space=pl.ANY))
+        operands.append(earlier)
     return pl.pallas_call(
-        functools.partial(far_kernel, kv_heads),
+        functools.partial(far_kernel, first_kv, kv_count),
         grid_spec=pltpu.PrefetchScalarGridSpec(
-            num_scalar_prefetch=2,
-            grid=(slots,),
-            in_specs=[
-                wide,
-                wide,
-                pl.BlockSpec((SEGMENT_TOKENS, 2 * STAT_HALF), lambda s, p, v: (s, 0)),
-                pl.BlockSpec((1, SEGMENT_TOKENS, kv_width), lambda s, p, v: (p[2 * s], 0, 0)),
-                pl.BlockSpec((1, SEGMENT_TOKENS, kv_width), lambda s, p, v: (p[2 * s + 1], 0, 0)),
-            ],
-            out_specs=wide,
+            num_scalar_prefetch=2, grid=(slots,), in_specs=in_specs, out_specs=wide
         ),
         out_shape=jax.ShapeDtypeStruct((tokens, width), jnp.bfloat16),
+        input_output_aliases=aliases,
         compiler_params=pltpu.CompilerParams(vmem_limit_bytes=VMEM_LIMIT),
         cost_estimate=pl.CostEstimate(
-            flops=8 * tokens * width * SEGMENT_TOKENS,
-            bytes_accessed=6 * tokens * width,
-            transcendentals=tokens * width * 2,
+            flops=8 * tokens * share * SEGMENT_TOKENS,
+            bytes_accessed=6 * tokens * share,
+            transcendentals=tokens * share * 2,
         ),
         name="far",
-    )(places, seen, tree_query, near, stats, gathered, gathered)
+    )(*operands)
 
 
 def trunk_call(start, trunk_query, key_all, value_all):
@@ -251,19 +262,22 @@
         jnp.concatenate([trunk_key, trunk_value], axis=1), "ctx", axis=0, tiled=True
     )
     key_all, value_all = trunk_both[:, :kv_width], trunk_both[:, kv_width:]
-    packed = jnp.concatenate(
-        [
-            tree_key.reshape(slots, SEGMENT_TOKENS, kv_width)[picked],
-            tree_value.reshape(slots, SEGMENT_TOKENS, kv_width)[picked],
-        ],
-        axis=2,
-    )
-    gathered = lax.all_gather(packed, "ctx", axis=0, tiled=True)
+    own_keys = tree_key.reshape(slots, SEGMENT_TOKENS, kv_width)[picked]
+    own_values = tree_value.reshape(slots, SEGMENT_TOKENS, kv_width)[picked]
+    kv_heads = kv_width // HEAD_SIZE
+    cuts = [0, kv_heads - 1, kv_heads] if kv_heads > 1 else [0, kv_heads]
+    gathered = []
+    for first, last in zip(cuts[:-1], cuts[1:]):
+        cols = slice(first * HEAD_SIZE, last * HEAD_SIZE)
+        packed = jnp.concatenate([own_keys[:, :, cols], own_values[:, :, cols]], axis=2)
+        gathered.append(lax.all_gather(packed, "ctx", axis=0, tiled=True))
 
     near, stats = near_call(tree_query, key_all, value_all, tree_key, tree_value)
     start = (me * trunk_query.shape[0]).astype(jnp.int32).reshape(1)
     trunk_out = trunk_call(start, trunk_query, key_all, value_all)
-    tree_out = far_call(places, seen, tree_query, near, stats, gathered)
+    tree_out = None
+    for first, pieces in zip(cuts[:-1], gathered):
+        tree_out = far_call(places, seen, tree_query, near, stats, pieces, first, tree_out)
     return trunk_out, tree_out
 
 

time: 451 us -> 388 us (0.86)
  waiting for transfers between devices: 200 us -> 135 us
    all_gather x1 -> x2, waiting for transfers between devices: 182 us -> 119 us  [local(): gathered.append(lax.all_gather(packed, 'ctx', axis=0, tiled=True))]
    pallas_call x1 -> x2, Pallas kernels: 113 us -> 115 us  [far_call(): pl.pallas_call(functools.partial(far_kernel, first_kv, kv_count), grid_sp...]
  transfers between devices with their start and end apart: 2 -> 3, of which waited for: 2 -> 3; matrix products, arithmetic and copies ran while one was open for 3% -> 3% of each run, Pallas kernels for 23% -> 46%
where the time goes in v2:
time: 388 us
  Pallas kernels  218 us (56%)
  waiting for transfers between devices  135 us (35%)
  local copies, waits for them, and re-layouts  15.3 us (4%)
  between operations  13.8 us (4%)
  other arithmetic  5.55 us (1%)
    all_gather x2, waiting for transfers between devices, local(): gathered.append(lax.all_gather(packed, 'ctx', axis=0, tiled=True))  119 us
    pallas_call x2, Pallas kernels, far_call(): pl.pallas_call(functools.partial(far_kernel, first_kv, kv_count), grid_sp...  115 us
    pallas_call x1, Pallas kernels, near_call(): pl.pallas_call(functools.partial(near_kernel, kv_heads), grid=(slots,), i...  99.4 us
    all_gather x1, waiting for transfers between devices, local(): lax.all_gather(jnp.concatenate([trunk_key, trunk_value], axis=1), 'ctx',...  16.1 us
  transfers between devices with their start and end apart: 3, of which 3 were waited for; matrix products, arithmetic and copies ran while one was open for 3% of the time, Pallas kernels for 46%

profile of v2, /device:TPU:0, one launch (start us, length us, event | category | flops | bytes accessed | tf_op | source)
XLA Modules:
  0.0 388.1 jit_solution(3750583928965778328)
XLA Ops:
  7.2 0.0 all-gather.4.cloned.1.call-start
  7.2 1.7 pad_maximum_fusion.2
  8.9 0.0 all-gather.4.cloned.1.call-update
  8.9 0.0 all-gather.8.cloned.1.call-start
  9.0 0.8 copy.16
  9.8 0.1 eq.65
  9.9 0.1 fusion
  10.0 0.2 select_reduce_fusion
  10.2 0.2 select_reduce_fusion.2
  10.4 3.7 gather_fusion.1
  14.2 0.0 copy-start.1
  14.2 1.7 copy-done.1
  15.9 2.0 gather_fusion
  17.9 0.0 slice-start
  17.9 0.0 slice-start.2
  17.9 1.4 slice-done
  19.3 0.5 slice-done.2
  19.9 2.0 pad_maximum_fusion
  21.9 0.0 slice-start.1
  21.9 0.0 slice-start.3
  21.9 0.0 all-gather.8.cloned.1.call-update
  21.9 0.0 copy-start.4
  21.9 0.0 all-gather.6.cloned.1.call-start
  22.0 1.0 slice-done.1
  22.9 0.2 slice-done.3
  23.1 0.0 copy-start.3
  23.1 1.1 pad_maximum_fusion.1
  24.2 0.0 all-gather.6.cloned.1.call-update
  24.3 0.0 copy-done.4
  24.3 0.1 constant_dynamic-slice_fusion
  24.4 0.1 copy.15
  24.5 0.1 eq.58
  24.6 0.2 select_reduce_fusion.1.place_ref
  24.7 16.1 %all-gather.4.cloned.1.call-done = bf16[512,1024]{1,0:T(8,128)(2,1)} async-done(((bf16[128,1024]{1,0:T(8,128)(2,1)}), bf16[512,1024]{1,0:T(8,128)(2,1)}) %all-gather.4.cloned.1.call-update) | async-done | bytes 1048592 | tf_op jit(solution)/shard_map/all_gather | solution.py:261
  40.8 0.0 copy-start.2
  40.8 1.4 fusion.4
  42.2 0.0 copy-done.3
  42.2 3.7 trunk.1
  46.0 0.0 copy-done.2
  46.0 99.4 %near.1 = (bf16[2560,4096]{1,0:T(8,128)(2,1)}, f32[2560,128]{1,0:T(8,128)S(1)}) custom-call(bf16[2560,4096]{1,0:T(8,128)(2,1)} %q_ref.7, bf16[512,512]{1,0:T(8,128)(2,1)S(1)} %get-tuple-element.7.kt_ref, bf16[512,512]{1,0:T(8,128)(2,1)S(1)} %get-tuple-element.6.vt_ref, bf16[2560,512]{1,0:T(8,128)(2,1)S(1)} %copy-done.2, bf16[2560,512]{1,0:T(8,128)(2,1)} %vs_ref.1), custom_call_target="tpu_custom_call" | custom-call | flops 26843545600 | bytes 41943040 | tf_op jit(solution)/shard_map/near/pallas_call | solution.py:153
  145.4 115.3 %all-gather.8.cloned.1.call-done.kv0_ref.kv1_ref = bf16[64,128,768]{2,1,0:T(8,128)(2,1)} async-done(((bf16[16,128,768]{2,1,0:T(8,128)(2,1)}), bf16[64,128,768]{2,1,0:T(8,128)(2,1)}) %all-gather.8.cloned.1.call-update) | async-done | bytes 12582928 | tf_op jit(solution)/shard_map/all_gather | solution.py:273
  260.7 76.8 %far.2.rest_0_ = bf16[2560,4096]{1,0:T(8,128)(2,1)} custom-call(s32[40]{0:T(128)S(1)} %select_reduce_fusion.1.place_ref, s32[40]{0:T(128)S(1)} %compare_convert_fusion.seen_ref, bf16[2560,4096]{1,0:T(8,128)(2,1)} %q_ref.7, bf16[2560,4096]{1,0:T(8,128)(2,1)} %get-tuple-element.4.near_ref, f32[2560,128]{1,0:T(8,128)S(1)} %get-tuple-element.5.stat_ref, ...), custom_call_target="tpu_custom_call" | custom-call | flops 8053063680 | bytes 47185920 | tf_op jit(solution)/shard_map/far/pallas_call | solution.py:193
  337.4 3.8 all-gather.6.cloned.1.call-done.kv0_ref.kv1_ref
  341.2 0.0 copy-start
  341.2 2.2 copy-done
  343.4 38.1 %far.3 = bf16[2560,4096]{1,0:T(8,128)(2,1)} custom-call(s32[40]{0:T(128)S(1)} %select_reduce_fusion.1.place_ref, s32[40]{0:T(128)S(1)} %compare_convert_fusion.seen_ref, bf16[2560,4096]{1,0:T(8,128)(2,1)} %q_ref.7, bf16[2560,4096]{1,0:T(8,128)(2,1)} %get-tuple-element.4.near_ref, ...), custom_call_target="tpu_custom_call", output_to_operand_aliasing={{}: (7, {})} | custom-call | flops 2684354560 | bytes 15728640 | tf_op jit(solution)/shard_map/far/pallas_call | solution.py:193
  (6 shorter events, 0.0 us)
Async XLA Ops:
  7.2 33.6 %all-gather.4.cloned.1.call-start = ((), (), s32[]{:S(2)}) async-start(), calls=%async_computation | async-start | bytes 1310720 | tf_op jit(solution)/shard_map/all_gather | solution.py:261
  8.9 251.7 %all-gather.8.cloned.1.call-start = ((), (), s32[]{:S(2)}) async-start(), calls=%async_computation.2 | async-start | bytes 15728640 | tf_op jit(solution)/shard_map/all_gather | solution.py:273
  14.2 1.7 copy-start.1
  17.9 1.4 slice-start
  17.9 1.9 slice-start.2
  21.9 1.0 slice-start.1
  21.9 1.2 slice-start.3
  21.9 2.4 copy-start.4
  21.9 319.3 %all-gather.6.cloned.1.call-start = ((), (), s32[]{:S(2)}) async-start(), calls=%async_computation.1 | async-start | bytes 5242880 | tf_op jit(solution)/shard_map/all_gather | solution.py:273
  23.1 19.1 %copy-start.3 = (bf16[128,4096]{1,0:T(8,128)(2,1)S(1)}, bf16[128,4096]{1,0:T(8,128)(2,1)}, u32[]{:S(2)}) copy-start(bf16[128,4096]{1,0:T(8,128)(2,1)} %q_ref.4) | copy-start | bytes 3145732
  40.8 5.2 %copy-start.2 = (bf16[2560,512]{1,0:T(8,128)(2,1)S(1)}, bf16[2560,512]{1,0:T(8,128)(2,1)}, u32[]{:S(2)}) copy-start(bf16[2560,512]{1,0:T(8,128)(2,1)} %ks_ref.1) | copy-start | bytes 7864324
  341.2 2.2 copy-start
Sparse Core Ops, SparseCore 0:
  10.1 30.6 all-gather.3
  42.9 217.6 all-gather.7
  262.3 78.9 all-gather.5

commit v3 on v2

--- a/solution.py
+++ b/solution.py
@@ -12,6 +12,7 @@
 SEGMENT_TOKENS = 128
 GROUP = 8
 ROW_HEADS = 2
+FAR_HEADS = 4
 STAT_WIDTH = 128
 MASKED = -1e30
 LOG2E_SCALE = math.log2(math.e) / math.sqrt(HEAD_SIZE)
@@ -99,21 +100,21 @@
         vcols = slice(width + j * HEAD_SIZE, width + (j + 1) * HEAD_SIZE)
         keys = jnp.concatenate([kv0_ref[0, :, cols], kv1_ref[0, :, cols]], axis=0)
         values = with_ones(jnp.concatenate([kv0_ref[0, :, vcols], kv1_ref[0, :, vcols]], axis=0))
-        for first in range(j * GROUP, (j + 1) * GROUP, ROW_HEADS):
-            queries = stack_heads(q_ref, first, ROW_HEADS)
+        for first in range(j * GROUP, (j + 1) * GROUP, FAR_HEADS):
+            queries = stack_heads(q_ref, first, FAR_HEADS)
             scores = scores_of(queries, keys) * LOG2E_SCALE + bar
             stat = first_kv * GROUP + first
             level = jnp.concatenate(
-                [stat_ref[:, stat + h : stat + h + 1] for h in range(ROW_HEADS)], axis=0
+                [stat_ref[:, stat + h : stat + h + 1] for h in range(FAR_HEADS)], axis=0
             )
             peak = jnp.maximum(level, jnp.max(scores, axis=1, keepdims=True))
             weights = jnp.exp2(scores - peak).astype(jnp.bfloat16)
             summed = jnp.dot(weights, values, preferred_element_type=jnp.float32)
             factor = jnp.exp2(level - peak)
-            near = stack_heads(near_ref, first, ROW_HEADS).astype(jnp.float32)
+            near = stack_heads(near_ref, first, FAR_HEADS).astype(jnp.float32)
             total = factor + summed[:, HEAD_SIZE:]
             out = ((factor * near + summed[:, :HEAD_SIZE]) / total).astype(jnp.bfloat16)
-            for h in range(ROW_HEADS):
+            for h in range(FAR_HEADS):
                 part = slice(h * SEGMENT_TOKENS, (h + 1) * SEGMENT_TOKENS)
                 head = first + h
                 o_ref[:, head * HEAD_SIZE : (head + 1) * HEAD_SIZE] = out[part]

time: 388 us -> 382 us (0.985)
  Pallas kernels: 218 us -> 194 us
  waiting for transfers between devices: 135 us -> 153 us
    pallas_call x2, Pallas kernels: 115 us -> 90.9 us  [far_call(): pl.pallas_call(functools.partial(far_kernel, first_kv, kv_count), grid_sp...]
    all_gather x2, waiting for transfers between devices: 119 us -> 137 us  [local(): gathered.append(lax.all_gather(packed, 'ctx', axis=0, tiled=True))]
  transfers between devices with their start and end apart: 3 -> 3, of which waited for: 3 -> 3; matrix products, arithmetic and copies ran while one was open for 3% -> 3% of each run, Pallas kernels for 46% -> 42%
where the time goes in v3:
time: 382 us
  Pallas kernels  194 us (51%)
  waiting for transfers between devices  153 us (40%)
  local copies, waits for them, and re-layouts  15.3 us (4%)
  between operations  13.8 us (4%)
  other arithmetic  5.55 us (1%)
    all_gather x2, waiting for transfers between devices, local(): gathered.append(lax.all_gather(packed, 'ctx', axis=0, tiled=True))  137 us
    pallas_call x1, Pallas kernels, near_call(): pl.pallas_call(functools.partial(near_kernel, kv_heads), grid=(slots,), i...  99.4 us
    pallas_call x2, Pallas kernels, far_call(): pl.pallas_call(functools.partial(far_kernel, first_kv, kv_count), grid_sp...  90.9 us
    all_gather x1, waiting for transfers between devices, local(): lax.all_gather(jnp.concatenate([trunk_key, trunk_value], axis=1), 'ctx',...  16.1 us
  transfers between devices with their start and end apart: 3, of which 3 were waited for; matrix products, arithmetic and copies ran while one was open for 3% of the time, Pallas kernels for 42%

profile of v3, /device:TPU:0, one launch (start us, length us, event | category | flops | bytes accessed | tf_op | source)
XLA Modules:
  0.0 382.0 jit_solution(17389186937657680138)
XLA Ops:
  7.2 0.0 all-gather.4.cloned.1.call-start
  7.2 1.7 pad_maximum_fusion.2
  8.9 0.0 all-gather.4.cloned.1.call-update
  8.9 0.0 all-gather.8.cloned.1.call-start
  9.0 0.8 copy.16
  9.8 0.1 eq.65
  9.9 0.1 fusion
  10.0 0.2 select_reduce_fusion
  10.2 0.2 select_reduce_fusion.2
  10.4 3.7 gather_fusion.1
  14.2 0.0 copy-start.1
  14.2 1.7 copy-done.1
  15.9 2.0 gather_fusion
  17.9 0.0 slice-start
  17.9 0.0 slice-start.2
  17.9 1.4 slice-done
  19.3 0.5 slice-done.2
  19.9 2.0 pad_maximum_fusion
  21.9 0.0 slice-start.1
  21.9 0.0 slice-start.3
  21.9 0.0 all-gather.8.cloned.1.call-update
  21.9 0.0 copy-start.4
  21.9 0.0 all-gather.6.cloned.1.call-start
  22.0 1.0 slice-done.1
  22.9 0.2 slice-done.3
  23.1 0.0 copy-start.3
  23.1 1.1 pad_maximum_fusion.1
  24.2 0.0 all-gather.6.cloned.1.call-update
  24.3 0.0 copy-done.4
  24.3 0.1 constant_dynamic-slice_fusion
  24.4 0.1 copy.15
  24.5 0.1 eq.58
  24.6 0.2 select_reduce_fusion.1.place_ref
  24.7 16.1 %all-gather.4.cloned.1.call-done = bf16[512,1024]{1,0:T(8,128)(2,1)} async-done(((bf16[128,1024]{1,0:T(8,128)(2,1)}), bf16[512,1024]{1,0:T(8,128)(2,1)}) %all-gather.4.cloned.1.call-update) | async-done | bytes 1048592 | tf_op jit(solution)/shard_map/all_gather | solution.py:262
  40.8 0.0 copy-start.2
  40.8 1.4 fusion.4
  42.2 0.0 copy-done.3
  42.2 3.7 trunk.1
  46.0 0.0 copy-done.2
  46.0 99.4 %near.1 = (bf16[2560,4096]{1,0:T(8,128)(2,1)}, f32[2560,128]{1,0:T(8,128)S(1)}) custom-call(bf16[2560,4096]{1,0:T(8,128)(2,1)} %q_ref.7, bf16[512,512]{1,0:T(8,128)(2,1)S(1)} %get-tuple-element.7.kt_ref, bf16[512,512]{1,0:T(8,128)(2,1)S(1)} %get-tuple-element.6.vt_ref, bf16[2560,512]{1,0:T(8,128)(2,1)S(1)} %copy-done.2, bf16[2560,512]{1,0:T(8,128)(2,1)} %vs_ref.1), custom_call_target="tpu_custom_call" | custom-call | flops 26843545600 | bytes 41943040 | tf_op jit(solution)/shard_map/near/pallas_call | solution.py:154
  145.4 115.3 %all-gather.8.cloned.1.call-done.kv0_ref.kv1_ref = bf16[64,128,768]{2,1,0:T(8,128)(2,1)} async-done(((bf16[16,128,768]{2,1,0:T(8,128)(2,1)}), bf16[64,128,768]{2,1,0:T(8,128)(2,1)}) %all-gather.8.cloned.1.call-update) | async-done | bytes 12582928 | tf_op jit(solution)/shard_map/all_gather | solution.py:274
  260.7 58.8 %far.2.rest_0_ = bf16[2560,4096]{1,0:T(8,128)(2,1)} custom-call(s32[40]{0:T(128)S(1)} %select_reduce_fusion.1.place_ref, s32[40]{0:T(128)S(1)} %compare_convert_fusion.seen_ref, bf16[2560,4096]{1,0:T(8,128)(2,1)} %q_ref.7, bf16[2560,4096]{1,0:T(8,128)(2,1)} %get-tuple-element.4.near_ref, f32[2560,128]{1,0:T(8,128)S(1)} %get-tuple-element.5.stat_ref, ...), custom_call_target="tpu_custom_call" | custom-call | flops 8053063680 | bytes 47185920 | tf_op jit(solution)/shard_map/far/pallas_call | solution.py:194
  319.5 21.7 %all-gather.6.cloned.1.call-done.kv0_ref.kv1_ref = bf16[64,128,256]{2,1,0:T(8,128)(2,1)} async-done(((bf16[16,128,256]{2,1,0:T(8,128)(2,1)}), bf16[64,128,256]{2,1,0:T(8,128)(2,1)}) %all-gather.6.cloned.1.call-update) | async-done | bytes 4194320 | tf_op jit(solution)/shard_map/all_gather | solution.py:274
  341.2 0.0 copy-start
  341.2 2.2 copy-done
  343.4 32.0 %far.3 = bf16[2560,4096]{1,0:T(8,128)(2,1)} custom-call(s32[40]{0:T(128)S(1)} %select_reduce_fusion.1.place_ref, s32[40]{0:T(128)S(1)} %compare_convert_fusion.seen_ref, bf16[2560,4096]{1,0:T(8,128)(2,1)} %q_ref.7, bf16[2560,4096]{1,0:T(8,128)(2,1)} %get-tuple-element.4.near_ref, ...), custom_call_target="tpu_custom_call", output_to_operand_aliasing={{}: (7, {})} | custom-call | flops 2684354560 | bytes 15728640 | tf_op jit(solution)/shard_map/far/pallas_call | solution.py:194
  (6 shorter events, 0.0 us)
Async XLA Ops:
  7.2 33.6 %all-gather.4.cloned.1.call-start = ((), (), s32[]{:S(2)}) async-start(), calls=%async_computation | async-start | bytes 1310720 | tf_op jit(solution)/shard_map/all_gather | solution.py:262
  8.9 251.7 %all-gather.8.cloned.1.call-start = ((), (), s32[]{:S(2)}) async-start(), calls=%async_computation.2 | async-start | bytes 15728640 | tf_op jit(solution)/shard_map/all_gather | solution.py:274
  14.2 1.7 copy-start.1
  17.9 1.4 slice-start
  17.9 1.9 slice-start.2
  21.9 1.0 slice-start.1
  21.9 1.2 slice-start.3
  21.9 2.4 copy-start.4
  21.9 319.3 %all-gather.6.cloned.1.call-start = ((), (), s32[]{:S(2)}) async-start(), calls=%async_computation.1 | async-start | bytes 5242880 | tf_op jit(solution)/shard_map/all_gather | solution.py:274
  23.1 19.1 %copy-start.3 = (bf16[128,4096]{1,0:T(8,128)(2,1)S(1)}, bf16[128,4096]{1,0:T(8,128)(2,1)}, u32[]{:S(2)}) copy-start(bf16[128,4096]{1,0:T(8,128)(2,1)} %q_ref.4) | copy-start | bytes 3145732
  40.8 5.2 %copy-start.2 = (bf16[2560,512]{1,0:T(8,128)(2,1)S(1)}, bf16[2560,512]{1,0:T(8,128)(2,1)}, u32[]{:S(2)}) copy-start(bf16[2560,512]{1,0:T(8,128)(2,1)} %ks_ref.1) | copy-start | bytes 7864324
  341.2 2.2 copy-start
Sparse Core Ops, SparseCore 0:
  10.1 30.6 all-gather.3
  42.9 217.6 all-gather.7
  262.3 78.9 all-gather.5
